TPU v7x, 128 devices: a whole 4x4x4 slice. The times are simulated.
128 devices in a mesh: row: 8 (over y, core), col: 16 (over x, z).
Axes of the slice: x: 4, y: 4, z: 4, core: 2. Of those that a mesh axis runs over, the one named last changes fastest.
Arguments:
- covariance: float32 [4, 4096, 2, 8192], P(None, 'row', None, 'col'), may hold values from 0 to 2, as said below
- band_mask: int32 [32, 32], replicated, may hold values from 0 to 1, as said below
Outputs:
- schur: float32 [4, 4096, 2, 8192], P(None, 'row', None, 'col')
- panels: float32 [4, 4096, 1024], P(None, 'row')
Inputs may be any that keep to these rules, and one draw needn't show every extreme that they name: band_mask is symmetric, holds 0 or 1, and is 1 wherever the two tile indices differ by at most 1 and wherever either tile index is below 2. covariance is symmetric, with 1 added on its diagonal; A is positive definite.
All inputs are finite; a program needn't handle non-finite values.
Results may differ from a plain program's by a relative error of at most 0.0003.
Values sent between devices are 32-bit elements; how exact they have to be, the bound alone decides.
A program may use at most 128 MiB of HBM per device.

v0:
```python
import jax
import jax.numpy as jnp
from jax import lax
from jax.sharding import PartitionSpec as P

TILE = 512


def from_root(value, axis, root):
    mine = lax.axis_index(axis) == root
    return lax.psum(jnp.where(mine, value, jnp.zeros_like(value)), axis)


def solve_below(factor, column, tile_ids, index):
    count = column.shape[0]
    rhs_block = jnp.transpose(column, (2, 0, 1)).reshape(TILE, count * TILE)
    solved = lax.linalg.triangular_solve(factor, rhs_block, left_side=True, lower=True)
    solved = jnp.transpose(solved.reshape(TILE, count, TILE), (1, 2, 0))
    chosen = tile_ids[:, None, None]
    return jnp.where(
        chosen > index, solved, jnp.where(chosen == index, factor[None], jnp.zeros_like(solved))
    )


def outer_update(target, row_part, col_part):
    return target - jnp.einsum("mab,ncb->manc", row_part, col_part, precision=lax.Precision.HIGHEST)


def body(covariance, band_mask):
    row_count = lax.axis_size("row")
    col_count = lax.axis_size("col")
    row_index = lax.axis_index("row")
    col_index = lax.axis_index("col")
    tile_total = band_mask.shape[0]
    row_tiles = tile_total // row_count
    col_tiles = tile_total // col_count
    row_ids = jnp.arange(row_tiles, dtype=jnp.int32) * row_count + row_index
    col_ids = jnp.arange(col_tiles, dtype=jnp.int32) * col_count + col_index
    keep_all = band_mask.astype(jnp.float32)
    keep_rows = lax.dynamic_index_in_dim(
        keep_all.reshape(row_tiles, row_count, tile_total), row_index, 1, keepdims=False
    )
    keep_local = lax.dynamic_index_in_dim(
        keep_rows.reshape(row_tiles, col_tiles, col_count), col_index, 2, keepdims=False
    )
    schur = covariance * keep_local[:, None, :, None]

    def to_columns(row_part):
        grouped = row_part.reshape(col_tiles, col_count // row_count, TILE, TILE)
        picked = lax.dynamic_index_in_dim(grouped, col_index // row_count, 1, keepdims=False)
        return from_root(picked, "row", col_index % row_count)

    def make_panel(column, column_step):
        diag_local = column[column_step // row_count]
        received = from_root(diag_local, "row", column_step % row_count)
        identity = jnp.eye(TILE, dtype=jnp.float32)
        diagonal = jnp.where(col_index == column_step % col_count, received, identity)
        factor = jnp.linalg.cholesky(diagonal)
        panel = solve_below(factor, column, row_ids, column_step)
        row_part = from_root(panel, "col", column_step % col_count)
        return (row_part, to_columns(row_part))

    rows_zero, cols_zero = make_panel(schur[:, :, 0, :], 0)
    schur = outer_update(schur, rows_zero, cols_zero)
    rows_one, cols_one = make_panel(schur[:, :, 0, :], 1)
    schur = outer_update(schur, rows_one, cols_one)
    row_keep = (row_ids >= 2).astype(jnp.float32)
    col_keep = (col_ids >= 2).astype(jnp.float32)
    schur = schur * row_keep[:, None, None, None] * col_keep[None, None, :, None]
    panels = jnp.concatenate([rows_zero, rows_one], axis=2)
    return (schur, panels)


def solution(mesh):
    return jax.shard_map(
        body,
        mesh=mesh,
        in_specs=(P(None, "row", None, "col"), P()),
        out_specs=(P(None, "row", None, "col"), P(None, "row", None)),
        check_vma=False,
    )
```

profile of v0, /device:TPU:45, one launch (start us, length us, event | category | flops | bytes accessed | tf_op | source)
XLA Modules:
  0.0 883.2 jit_solution(13052598460974647819)
XLA Ops:
  8.3 13.1 %copy.18 = f32[4,512,2,512]{1,3,2,0:T(8,128)} copy(f32[4,512,2,512]{3,2,1,0:T(2,128)} %param.5) | data formatting | bytes 16777216 | tf_op args[0]
  40.6 50.2 %all-reduce.8.cloned.1.call-done = f32[512,512]{0,1:T(8,128)} async-done(((f32[512,512]{0,1:T(8,128)}), f32[512,512]{0,1:T(8,128)}) %all-reduce.8.cloned.1.call-update) | async-done | bytes 1048592 | tf_op jit(solution)/shard_map/psum | solution.py:11
  92.2 11.7 %cholesky.286 = f32[128,128]{1,0:T(8,128)S(1)} custom-call(f32[128,128]{1,0:T(8,128)S(1)} %cholesky.426), custom_call_target="Cholesky" | custom-call | tf_op jit(solution)/shard_map/jit(cholesky)/cholesky | solution.py:58
  104.0 9.8 %custom-call.27 = f32[1,128,128]{1,2,0:T(8,128)S(1)} custom-call(f32[1,128,128]{2,1,0:T(8,128)S(1)} %get-tuple-element.67), custom_call_target="InvertDiagBlocksLowerTriangular" | custom-call | tf_op jit(solution)/shard_map/jit(cholesky)/cholesky | solution.py:58
  114.6 11.7 %cholesky.305 = f32[128,128]{1,0:T(8,128)S(1)} custom-call(f32[128,128]{1,0:T(8,128)S(1)} %cholesky.430), custom_call_target="Cholesky" | custom-call | tf_op jit(solution)/shard_map/jit(cholesky)/cholesky | solution.py:58
  126.3 10.2 %custom-call.28 = f32[1,128,128]{1,2,0:T(8,128)S(1)} custom-call(f32[1,128,128]{2,1,0:T(8,128)S(1)} %get-tuple-element.64), custom_call_target="InvertDiagBlocksLowerTriangular" | custom-call | tf_op jit(solution)/shard_map/jit(cholesky)/cholesky | solution.py:58
  137.3 11.7 %cholesky.326 = f32[128,128]{1,0:T(8,128)S(1)} custom-call(f32[128,128]{1,0:T(8,128)S(1)} %cholesky.435), custom_call_target="Cholesky" | custom-call | tf_op jit(solution)/shard_map/jit(cholesky)/cholesky | solution.py:58
  160.1 11.7 %cholesky.343 = f32[128,128]{1,0:T(8,128)S(1)} custom-call(f32[128,128]{1,0:T(8,128)S(1)} %convolution_subtract_fusion.9), custom_call_target="Cholesky" | custom-call | tf_op jit(solution)/shard_map/jit(cholesky)/cholesky | solution.py:58
  184.1 39.3 %custom-call.30 = f32[4,128,128]{1,2,0:T(8,128)S(1)} custom-call(f32[4,128,128]{2,1,0:T(8,128)S(1)} %get-tuple-element.18), custom_call_target="InvertDiagBlocksLowerTriangular" | custom-call | tf_op jit(solution)/shard_map/triangular_solve/custom-call.3 | solution.py:17
  254.2 105.8 %all-reduce.10.cloned.1.call-done = f32[4,512,512]{2,1,0:T(8,128)} async-done(((f32[4,512,512]{2,1,0:T(8,128)}), f32[4,512,512]{2,1,0:T(8,128)}) %all-reduce.10.cloned.1.call-update) | async-done | bytes 4194320 | tf_op jit(solution)/shard_map/psum | solution.py:11
  363.3 62.8 %all-reduce.12.cloned.1.call-done = f32[2,512,512]{2,1,0:T(8,128)} async-done(((f32[2,512,512]{2,1,0:T(8,128)}), f32[2,512,512]{2,1,0:T(8,128)}) %all-reduce.12.cloned.1.call-update) | async-done | bytes 2097168 | tf_op jit(solution)/shard_map/psum | solution.py:11
  426.1 16.9 %fusion.18 = f32[4,512,2,512]{1,3,2,0:T(8,128)S(1)} fusion(f32[4,512,2,512]{1,3,2,0:T(8,128)} %copy-done.1, f32[4,512,512]{2,1,0:T(8,128)} %all-reduce.10.cloned.1.call-done, f32[2,512,512]{2,1,0:T(8,128)} %all-reduce.12.cloned.1.call-done), kind=kOutput, calls=%fused_computation.29 | convolution fusion | flops 12886999040 | bytes 23068672 | tf_op jit(solution)/shard_map/mab,ncb->manc/dot_general | solution.py:26
  457.8 51.6 %all-reduce.14.cloned.1.call-done = f32[512,512]{0,1:T(8,128)} async-done(((f32[512,512]{0,1:T(8,128)}), f32[512,512]{0,1:T(8,128)}) %all-reduce.14.cloned.1.call-update) | async-done | bytes 1048592 | tf_op jit(solution)/shard_map/psum | solution.py:11
  510.9 11.7 %cholesky.358 = f32[128,128]{1,0:T(8,128)S(1)} custom-call(f32[128,128]{1,0:T(8,128)S(1)} %cholesky.439), custom_call_target="Cholesky" | custom-call | tf_op jit(solution)/shard_map/jit(cholesky)/cholesky | solution.py:58
  523.3 9.8 %custom-call.31 = f32[1,128,128]{1,2,0:T(8,128)S(1)} custom-call(f32[1,128,128]{2,1,0:T(8,128)S(1)} %get-tuple-element.57), custom_call_target="InvertDiagBlocksLowerTriangular" | custom-call | tf_op jit(solution)/shard_map/jit(cholesky)/cholesky | solution.py:58
  533.9 11.7 %cholesky.377 = f32[128,128]{1,0:T(8,128)S(1)} custom-call(f32[128,128]{1,0:T(8,128)S(1)} %cholesky.443), custom_call_target="Cholesky" | custom-call | tf_op jit(solution)/shard_map/jit(cholesky)/cholesky | solution.py:58
  546.2 10.0 %custom-call.32 = f32[1,128,128]{1,2,0:T(8,128)S(1)} custom-call(f32[1,128,128]{2,1,0:T(8,128)S(1)} %get-tuple-element.54), custom_call_target="InvertDiagBlocksLowerTriangular" | custom-call | tf_op jit(solution)/shard_map/jit(cholesky)/cholesky | solution.py:58
  556.9 11.7 %cholesky.398 = f32[128,128]{1,0:T(8,128)S(1)} custom-call(f32[128,128]{1,0:T(8,128)S(1)} %cholesky.448), custom_call_target="Cholesky" | custom-call | tf_op jit(solution)/shard_map/jit(cholesky)/cholesky | solution.py:58
  579.7 11.7 %cholesky.415 = f32[128,128]{1,0:T(8,128)S(1)} custom-call(f32[128,128]{1,0:T(8,128)S(1)} %convolution_subtract_fusion.8), custom_call_target="Cholesky" | custom-call | tf_op jit(solution)/shard_map/jit(cholesky)/cholesky | solution.py:58
  602.7 39.3 %custom-call.34 = f32[4,128,128]{1,2,0:T(8,128)S(1)} custom-call(f32[4,128,128]{2,1,0:T(8,128)S(1)} %get-tuple-element.19), custom_call_target="InvertDiagBlocksLowerTriangular" | custom-call | tf_op jit(solution)/shard_map/triangular_solve/custom-call.3 | solution.py:17
  672.8 105.8 %all-reduce.16.cloned.1.call-done = f32[4,512,512]{2,1,0:T(8,128)} async-done(((f32[4,512,512]{2,1,0:T(8,128)}), f32[4,512,512]{2,1,0:T(8,128)}) %all-reduce.16.cloned.1.call-update) | async-done | bytes 4194320 | tf_op jit(solution)/shard_map/psum | solution.py:11
  790.1 54.5 %all-reduce.18.cloned.1.call-done = f32[2,512,512]{2,1,0:T(8,128)} async-done(((f32[2,512,512]{2,1,0:T(8,128)}), f32[2,512,512]{2,1,0:T(8,128)}) %all-reduce.18.cloned.1.call-update) | async-done | bytes 2097168 | tf_op jit(solution)/shard_map/psum | solution.py:11
  844.7 18.1 %multiply_multiply_fusion = f32[4,512,2,512]{1,3,2,0:T(8,128)} fusion(f32[4,512,2,512]{1,3,2,0:T(8,128)} %copy-done, f32[2]{0:T(128)S(1)} %compare_convert_fusion, f32[4]{0:T(128)S(1)} %compare_convert_fusion.1, f32[4,512,512]{2,1,0:T(8,128)} %all-reduce.16.cloned.1.call-done, f32[2,512,512]{2,1,0:T(8,128)} %all-reduce.18.cloned.1.call-done), kind=kOutput, calls=%fused_computation.5 | convolution fusion | flops 12891193344 | bytes 23068696 | tf_op jit(solution)/shard_map/mab,ncb->manc/dot_general | solution.py:26
  862.8 13.1 %copy.29 = f32[4,512,2,512]{3,2,1,0:T(2,128)} copy(f32[4,512,2,512]{1,3,2,0:T(8,128)} %multiply_multiply_fusion) | data formatting | bytes 16777216
  (139 shorter events, 174.4 us)
Async XLA Ops:
  7.2 83.6 %all-reduce.8.cloned.1.call-start = ((), (), s32[]{:S(2)}) async-start(), calls=%async_computation | async-start | bytes 2097152 | tf_op jit(solution)/shard_map/psum | solution.py:11
  25.9 3.4 copy-start.1
  30.4 329.6 %all-reduce.10.cloned.1.call-start = ((), (), s32[]{:S(2)}) async-start(), calls=%async_computation.1 | async-start | bytes 8388608 | tf_op jit(solution)/shard_map/psum | solution.py:11
  90.8 1.2 copy-start.4
  223.5 6.6 copy-start.2
  254.1 172.0 %all-reduce.12.cloned.1.call-start = ((), (), s32[]{:S(2)}) async-start(), calls=%async_computation.2 | async-start | bytes 4194304 | tf_op jit(solution)/shard_map/psum | solution.py:11
  363.2 146.2 %all-reduce.14.cloned.1.call-start = ((), (), s32[]{:S(2)}) async-start(), calls=%async_computation.3 | async-start | bytes 2097152 | tf_op jit(solution)/shard_map/psum | solution.py:11
  443.0 3.4 copy-start
  447.5 331.1 %all-reduce.16.cloned.1.call-start = ((), (), s32[]{:S(2)}) async-start(), calls=%async_computation.4 | async-start | bytes 8388608 | tf_op jit(solution)/shard_map/psum | solution.py:11
  509.4 1.2 copy-start.5
  642.0 6.6 copy-start.3
  672.7 172.0 %all-reduce.18.cloned.1.call-start = ((), (), s32[]{:S(2)}) async-start(), calls=%async_computation.5 | async-start | bytes 4194304 | tf_op jit(solution)/shard_map/psum | solution.py:11
Sparse Core Ops, SparseCore 0:
  30.5 60.1 all-reduce.7
  254.3 105.7 all-reduce.9
  363.3 62.7 all-reduce.11
  447.6 61.7 all-reduce.13
  672.8 105.7 all-reduce.15
  781.9 62.7 all-reduce.17
where the time goes:
time: 892 us; the launch traced here: 883 us
  waiting for transfers between devices  431 us (48%)
  other arithmetic  275 us (31%)
  local copies, waits for them, and re-layouts  82.3 us (9%)
  matrix products  74.4 us (8%)
  between operations  20.1 us (2%)
    psum x6, waiting for transfers between devices, from_root(): return lax.psum(jnp.where(mine, value, jnp.zeros_like(value)), axis)  431 us
    another operation x29, other arithmetic, make_panel(): factor = jnp.linalg.cholesky(diagonal)  158 us
    another operation x7, other arithmetic, solve_below(): lax.linalg.triangular_solve(factor, rhs_block, left_side=True, lower=True)  84.2 us
    another operation x14, matrix products, solve_below(): lax.linalg.triangular_solve(factor, rhs_block, left_side=True, lower=True)  35.6 us
    dot_general x2, matrix products, outer_update(): jnp.einsum('mab,ncb->manc', row_part, col_part, precision=lax.Precision.H...  35 us
    unnamed x14, local copies, waits for them, and re-layouts  34.5 us
    another operation x28, local copies, waits for them, and re-layouts, solve_below(): lax.linalg.triangular_solve(factor, rhs_block, left_side=True, lower=True)  20.8 us
    transpose x4, local copies, waits for them, and re-layouts, solve_below(): rhs_block = jnp.transpose(column, (2, 0, 1)).reshape(TILE, count * TILE)  20.3 us
  transfers between devices with their start and end apart: 6, of which 6 were waited for; matrix products, arithmetic and copies ran while one was open for 3% of the time, Pallas kernels for 0%

commit v1 on v0

v1 whole, which is shorter than its diff:
```python
import functools

import jax
import jax.numpy as jnp
from jax import lax
from jax.experimental import pallas as pl
from jax.experimental.pallas import tpu as pltpu
from jax.sharding import PartitionSpec as P

TILE = 512
B = 128
NB = TILE // B
F32 = jnp.float32
BF16 = jnp.bfloat16
MESH = pl.DeviceIdType.MESH
HIGH = lax.Precision.HIGHEST

TREE_PARENT = {
    4: (0, 0), 7: (4, 3), 8: (4, 0), 5: (4, 1), 11: (7, 0), 6: (7, 3), 1: (5, 2), 3: (7, 2),
    9: (8, 1), 12: (8, 0), 10: (9, 1), 2: (6, 2), 13: (9, 0), 15: (11, 0), 14: (10, 0),
}
TREE_DEPTH = {0: 0, 4: 1, 7: 2, 8: 2, 5: 2, 11: 3, 6: 3, 1: 3, 3: 3, 9: 3, 12: 3, 10: 4, 2: 4, 13: 4, 15: 4, 14: 5}
MAX_DEPTH = 5
CHUNKS = 16
CROWS = TILE // CHUNKS
TCHUNKS = 8
TROWS = TILE // TCHUNKS
WROWS = B // 4


def factor_block(rows):
    n = len(rows)
    x = list(rows)
    sub = lax.broadcasted_iota(jnp.int32, (8, B), 0)
    lane = lax.broadcasted_iota(jnp.int32, (8, B), 1)
    for s in range(n):
        g0 = x[s]
        inside = (lane >= 8 * s) & (lane < 8 * s + 8)
        cols = [jnp.broadcast_to(g0[:, 8 * s + j : 8 * s + j + 1], (8, B)) for j in range(8)]
        a = [[jnp.broadcast_to(cols[j][i : i + 1, :], (8, B)) if i >= j else None for j in range(8)] for i in range(8)]
        gz = jnp.where(inside, (lane - 8 * s == sub).astype(F32), g0)
        g = [jnp.broadcast_to(gz[i : i + 1, :], (8, B)) for i in range(8)]
        l = [[None] * 8 for _ in range(8)]
        r = [None] * 8
        u = [None] * 8
        for j in range(8):
            r[j] = lax.rsqrt(a[j][j])
            u[j] = g[j] * r[j]
            for i in range(j + 1, 8):
                l[i][j] = a[i][j] * r[j]
            for i in range(j + 1, 8):
                for m in range(j + 1, i + 1):
                    a[i][m] = a[i][m] - l[i][j] * l[m][j]
                g[i] = g[i] - l[i][j] * u[j]
        out = u[0]
        for j in range(1, 8):
            out = jnp.where(sub == j, u[j], out)
        for t in range(s + 1, n):
            c = [jnp.broadcast_to(x[t][:, 8 * s + j : 8 * s + j + 1], (8, B)) for j in range(8)]
            acc = jnp.where(inside, 0.0, x[t])
            for j in range(8):
                cj = c[j] * r[j]
                acc = acc - cj * u[j]
                for m in range(j + 1, 8):
                    c[m] = c[m] - l[m][j] * cj
            x[t] = acc
        x[s] = out
    return jnp.concatenate(x, axis=0)


def dot_nn(a, b):
    return jnp.dot(a, b, precision=HIGH, preferred_element_type=F32)


def dot_nt(a, b):
    return lax.dot_general(a, b, (((1,), (1,)), ((), ())), precision=HIGH, preferred_element_type=F32)


def factor_tile(m, w, base, publish):
    rr = lax.broadcasted_iota(jnp.int32, (B, B), 0)
    cc = lax.broadcasted_iota(jnp.int32, (B, B), 1)
    cw = lax.broadcasted_iota(jnp.int32, (B, TILE), 1)

    def step(k, _):
        o = pl.multiple_of(k * B, B)
        rows = [m[pl.ds(pl.multiple_of(o + 8 * s, 8), 8), pl.ds(o, B)] for s in range(B // 8)]
        inv = jnp.where(cc <= rr, factor_block(rows), 0.0)
        inside = (cw >= o) & (cw < o + B)
        row = dot_nn(inv, m[pl.ds(o, B), :])
        row = jnp.where(inside, jnp.concatenate([inv] * NB, axis=1), row)
        m[pl.ds(o, B), :] = row
        w[pl.ds(pl.multiple_of(base + o, B), B), :] = jnp.where(cw < o + B, row, 0.0)
        publish(k)

        def update(i, _):
            oi = pl.multiple_of(i * B, B)
            left = dot_nt(m[pl.ds(oi, B), pl.ds(o, B)], inv)
            old = jnp.where(inside, 0.0, m[pl.ds(oi, B), :])
            m[pl.ds(oi, B), :] = old - dot_nn(left, m[pl.ds(o, B), :])
            return 0

        lax.fori_loop(k + 1, NB, update, 0)
        return 0

    lax.fori_loop(0, NB, step, 0)


def any_of(value, options):
    hit = value == options[0]
    for option in options[1:]:
        hit = hit | (value == option)
    return hit


def exchange_kernel(
    x0, x1, cbuf, tbuf, wout, m, amat, w, csend, crecv, tsend, trecv, wsend, wrecv, asend, arecv, lsem
):
    r = lax.axis_index("row")
    c = lax.axis_index("col")
    y, core = r // 2, r % 2
    x, z = c // 4, c % 4
    sibling = (r + 1 - 2 * core, c)
    around = [
        (r, ((x + 1) % 4) * 4 + z),
        (r, x * 4 + (z + 1) % 4),
        (r, ((x + 3) % 4) * 4 + z),
        (r, x * 4 + (z + 3) % 4),
    ]
    y_next = ((r + 2) % 8, c)
    y_prev = ((r + 6) % 8, c)
    root = (r == 0) & (c == 0)
    proxy = (r == 1) & (c == 0)
    near_root = (r == 0) & any_of(c, (1, 3, 4, 12))
    has_a11 = (r == 1) & (c == 1)

    bar = pltpu.get_barrier_semaphore()
    for dev in around + [y_next, y_prev, sibling]:
        pl.semaphore_signal(bar, inc=1, device_id=dev, device_id_type=MESH)

    @pl.when(near_root)
    def _():
        pl.semaphore_signal(bar, inc=1, device_id=(1, 0), device_id_type=MESH)

    @pl.when(proxy)
    def _():
        for col in (1, 3, 4, 12):
            pl.semaphore_signal(bar, inc=1, device_id=(0, col), device_id_type=MESH)

    @pl.when(has_a11)
    def _():
        pl.semaphore_signal(bar, inc=1, device_id=(0, 0), device_id_type=MESH)

    @pl.when(root)
    def _():
        pl.semaphore_signal(bar, inc=1, device_id=(1, 1), device_id_type=MESH)

    extra = near_root.astype(jnp.int32) + 4 * proxy.astype(jnp.int32) + has_a11.astype(jnp.int32) + root.astype(jnp.int32)
    pl.semaphore_wait(bar, 7 + extra)

    a10 = pltpu.make_async_remote_copy(
        x0.at[0], amat.at[0], asend.at[0], arecv.at[0], device_id=(0, 0), device_id_type=MESH
    )
    a11 = pltpu.make_async_remote_copy(
        x0.at[0], amat.at[1], asend.at[1], arecv.at[1], device_id=(0, 0), device_id_type=MESH
    )

    @pl.when(proxy)
    def _():
        a10.start()

    @pl.when(has_a11)
    def _():
        a11.start()

    first = pltpu.make_async_copy(x0.at[0], m, lsem.at[0])

    @pl.when(root)
    def _():
        first.start()

    place = []
    for s in range(2):
        zr = (z + 4 - s) % 4
        nx, nz = (4 - x) % 4, (4 - zr) % 4
        for q in range(4):
            a, b = ((x, zr), (zr, nx), (nx, nz), (nz, x))[q]
            node = 4 * a + b
            depth = jnp.int32(0)
            for k, v in TREE_DEPTH.items():
                depth = jnp.where(node == k, v, depth)
            flags = []
            for d in range(4):
                senders = [p for p, pd in TREE_PARENT.values() if pd == d]
                flags.append(any_of(node, sorted(senders)) if senders else None)
            place.append((node, depth, flags))

    def crow(chunk):
        return pl.ds(pl.multiple_of(chunk * CROWS, CROWS), CROWS)

    def csend_to(src, slot, dst_slot, d, target, chunk):
        return pltpu.make_async_remote_copy(
            src.at[crow(chunk)],
            cbuf.at[dst_slot, crow(chunk)],
            csend.at[slot, d],
            crecv.at[dst_slot, chunk],
            device_id=target,
            device_id_type=MESH,
        )

    def to_proxy(s, d, q):
        col = around[(d + q) % 4][1]
        return (r == 0) & (col == 0) if s == 1 else None

    def forward(src, s, q, slot, dst_slot, row, chunk, redirect):
        node, depth, flags = place[4 * s + q]
        for d in range(4):
            if flags[d] is None:
                continue
            col = around[(d + q) % 4][1]
            if redirect:
                away = (col == 0) & (r == 0)
                row_d = jnp.where(away, 1, row)
                slot_d = jnp.where(away, 8 + q, dst_slot)
            else:
                row_d, slot_d = row, dst_slot

            @pl.when(flags[d])
            def _():
                csend_to(src, slot, slot_d, d, (row_d, col), chunk).start()

    source = [c == 0, c == 1]

    def send_all(s):
        def go(chunk, _):
            for q in range(4):
                forward(x0.at[q], s, q, 4 * s + q, 4 * s + q, r, chunk, s == 1)
            return 0

        lax.fori_loop(0, CHUNKS, go, 0)

    def trow(chunk):
        return pl.ds(pl.multiple_of(chunk * TROWS, TROWS), TROWS)

    t_on = [y < 3, y != 1]
    t_dev = [y_next, y_prev]
    t_depth = [y, (4 - y) % 4]
    t_source = y == 0

    def t_forward(src, t, chunk):
        @pl.when(t_on[t])
        def _():
            pltpu.make_async_remote_copy(
                src.at[trow(chunk)], tbuf.at[core, t, trow(chunk)], tsend.at[t, 0], trecv.at[core, t, chunk],
                device_id=t_dev[t], device_id_type=MESH,
            ).start()

        pltpu.make_async_remote_copy(
            src.at[trow(chunk)], tbuf.at[core, t, trow(chunk)], tsend.at[t, 1], trecv.at[core, t, chunk],
            device_id=sibling, device_id_type=MESH,
        ).start()

    t_src = [x0.at[0], x1]

    @pl.when(t_source)
    def _():
        def go(chunk, _):
            for t in range(2):
                t_forward(t_src[t], t, chunk)
            return 0

        lax.fori_loop(0, TCHUNKS, go, 0)
        for t in range(2):
            pltpu.make_async_copy(t_src[t], tbuf.at[core, t], lsem.at[1 + t]).start()

    for s in range(2):

        @pl.when(source[s])
        def _():
            send_all(s)
            for q in range(4):
                pltpu.make_async_copy(x0.at[q], cbuf.at[4 * s + q], lsem.at[3 + q]).start()

    w_on = []
    for q in range(4):
        _, _, flags = place[q]
        on = [(flags[d] & (y == 0), around[(d + q) % 4]) if flags[d] is not None else None for d in range(4)]
        if q % 2 == 0:
            on.append((y < 3, y_next))
        else:
            on.append((y != 1, y_prev))
        on.append((core == 0, sibling))
        w_on.append(on)

    def w_rows(block, q):
        return pl.ds(pl.multiple_of(block * B + q * WROWS, WROWS), WROWS)

    def w_forward(block, q):
        for d, entry in enumerate(w_on[q]):
            if entry is None:
                continue
            flag, dev = entry

            @pl.when(flag & (core == 0))
            def _():
                pltpu.make_async_remote_copy(
                    w.at[w_rows(block, q)], w.at[w_rows(block, q)], wsend.at[q, d], wrecv.at[block, q],
                    device_id=dev, device_id_type=MESH,
                ).start()

    def w_wait(block, q):
        pltpu.make_async_copy(w.at[w_rows(block, q)], w.at[w_rows(block, q)], wrecv.at[block, q]).wait()

    def w_pass(mat):
        def go(k, _):
            for q in range(4):
                w_wait(mat * NB + k, q)
                w_forward(mat * NB + k, q)
            return 0

        lax.fori_loop(0, NB, go, 0)

    def c_wait(slot, chunk):
        pltpu.make_async_copy(cbuf.at[slot, crow(chunk)], cbuf.at[slot, crow(chunk)], crecv.at[slot, chunk]).wait()

    def t_wait(k, t, chunk):
        pltpu.make_async_copy(tbuf.at[k, t, trow(chunk)], tbuf.at[k, t, trow(chunk)], trecv.at[k, t, chunk]).wait()

    @pl.when(root)
    def _():
        first.wait()

        def publish(base):
            def go(k):
                for q in range(4):
                    w_forward(base + k, q)

            return go

        factor_tile(m, w, 0, publish(0))
        a10.wait_recv()
        left = dot_nt(amat[0], w[0:TILE, :])
        w[TILE : 2 * TILE, :] = left
        for k in range(NB):
            publish(NB)(k)
        a11.wait_recv()
        m[...] = amat[1] - dot_nt(left, left)
        factor_tile(m, w, 2 * TILE, publish(2 * NB))
        for q in range(4):

            def drain(chunk, _):
                c_wait(4 + q, chunk)
                return 0

            lax.fori_loop(0, CHUNKS, drain, 0)

    @pl.when(jnp.logical_not(root))
    def _():
        def go(k, _):
            for t in range(2):
                chunk = k - t_depth[t]

                @pl.when((chunk >= 0) & (chunk < TCHUNKS) & (y != 0))
                def _():
                    t_wait(core, t, chunk)
                    t_forward(tbuf.at[core, t], t, chunk)

            for s in range(2):
                for q in range(4):
                    _, depth, _ = place[4 * s + q]
                    chunk = k - depth

                    @pl.when((chunk >= 0) & (chunk < CHUNKS) & jnp.logical_not(source[s]))
                    def _():
                        c_wait(4 * s + q, chunk)
                        forward(cbuf.at[4 * s + q], s, q, 4 * s + q, 4 * s + q, r, chunk, s == 1)

                    if s == 1:

                        @pl.when((chunk >= 0) & (chunk < CHUNKS) & proxy)
                        def _():
                            c_wait(8 + q, chunk)
                            csend_to(cbuf.at[8 + q], 8 + q, 4 + q, 4, (0, 0), chunk).start()
                            forward(cbuf.at[8 + q], s, q, 8 + q, 4 + q, 0, chunk, False)

            @pl.when(k == CHUNKS - 1)
            def _():
                w_pass(0)

            @pl.when(k == CHUNKS + 1)
            def _():
                w_pass(1)

            return 0

        lax.fori_loop(0, CHUNKS + MAX_DEPTH, go, 0)
        w_pass(2)

    for t in range(2):

        def drain_t(chunk, _):
            t_wait(1 - core, t, chunk)
            return 0

        lax.fori_loop(0, TCHUNKS, drain_t, 0)

    out = pltpu.make_async_copy(w, wout, lsem.at[7])
    out.start()

    for slot in range(12):
        s = 0 if slot < 4 else 1
        q = slot % 4
        _, _, flags = place[4 * s + q]
        for d in range(5):
            flag = jnp.bool_(True) if d == 4 else flags[d]
            if flag is None or (d == 4 and slot < 8):
                continue
            if slot >= 8:
                flag = flag & proxy
            elif s == 1:
                flag = flag & jnp.logical_not(root)

            @pl.when(flag)
            def _():
                pltpu.make_async_copy(cbuf.at[slot], cbuf.at[slot], csend.at[slot, d]).wait()

    for t in range(2):

        @pl.when(t_on[t])
        def _():
            pltpu.make_async_copy(tbuf.at[0, t], tbuf.at[0, t], tsend.at[t, 0]).wait()

        pltpu.make_async_copy(tbuf.at[0, t], tbuf.at[0, t], tsend.at[t, 1]).wait()

    for q in range(4):
        for d, entry in enumerate(w_on[q]):
            if entry is None:
                continue

            @pl.when(entry[0] & (core == 0))
            def _():
                rows = 3 * NB * WROWS
                pltpu.make_async_copy(w.at[0:rows], w.at[0:rows], wsend.at[q, d]).wait()

    @pl.when(t_source)
    def _():
        for t in range(2):
            pltpu.make_async_copy(t_src[t], tbuf.at[core, t], lsem.at[1 + t]).wait()

    for s in range(2):

        @pl.when(source[s])
        def _():
            for q in range(4):
                pltpu.make_async_copy(x0.at[q], cbuf.at[4 * s + q], lsem.at[3 + q]).wait()

    @pl.when(proxy)
    def _():
        a10.wait_send()

    @pl.when(has_a11)
    def _():
        a11.wait_send()

    out.wait()


def exchange(x0, x1):
    any_space = pl.BlockSpec(memory_space=pl.ANY)
    dma = pltpu.SemaphoreType.DMA
    return pl.pallas_call(
        exchange_kernel,
        out_shape=(
            jax.ShapeDtypeStruct((12, TILE, TILE), F32),
            jax.ShapeDtypeStruct((2, 2, TILE, TILE), F32),
            jax.ShapeDtypeStruct((3 * TILE, TILE), F32),
        ),
        in_specs=[any_space, any_space],
        out_specs=(any_space, any_space, any_space),
        scratch_shapes=[
            pltpu.VMEM((TILE, TILE), F32),
            pltpu.VMEM((2, TILE, TILE), F32),
            pltpu.VMEM((3 * TILE, TILE), F32),
            dma((12, 5)),
            dma((12, CHUNKS)),
            dma((2, 2)),
            dma((2, 2, TCHUNKS)),
            dma((4, 6)),
            dma((3 * NB, 4)),
            dma((2,)),
            dma((2,)),
            dma((8,)),
        ],
        compiler_params=pltpu.CompilerParams(
            collective_id=0, has_side_effects=True, vmem_limit_bytes=48 * 2**20
        ),
        name="exchange",
    )(x0, x1)


def split(a):
    hi = a.astype(BF16)
    return hi, (a - hi.astype(F32)).astype(BF16)


def mm(a, b):
    return jnp.dot(a, b, preferred_element_type=F32)


def mm_t(a, b):
    return lax.dot_general(a, b, (((1,), (1,)), ((), ())), preferred_element_type=F32)


def product(a, b, dot):
    return dot(a[0], b[0]) + (dot(a[0], b[1]) + dot(a[1], b[0]))


def finish_kernel(keep, cov, c0, c1, tb, wo, schur, panel, wh, wl, pth, ptl, ph, plo):
    q = pl.program_id(0)
    r = lax.axis_index("row")
    c = lax.axis_index("col")
    i_tile = q * 8 + r

    @pl.when(q == 0)
    def _():
        hi, lo = split(wo[...])
        wh[...] = hi
        wl[...] = lo
        w00 = (wh[0:TILE], wl[0:TILE])
        l10 = (wh[TILE : 2 * TILE], wl[TILE : 2 * TILE])
        w11 = (wh[2 * TILE :], wl[2 * TILE :])
        for t in range(2):
            cols = slice(t * TILE, (t + 1) * TILE)
            p0 = split(product(w00, split(tb[0, t]), mm))
            pth[0:TILE, cols] = p0[0]
            ptl[0:TILE, cols] = p0[1]
            rest = tb[1, t] - product(l10, p0, mm)
            p1 = split(product(w11, split(rest), mm))
            pth[TILE:, cols] = p1[0]
            ptl[TILE:, cols] = p1[1]

    w00 = (wh[0:TILE], wl[0:TILE])
    l10 = (wh[TILE : 2 * TILE], wl[TILE : 2 * TILE])
    w11 = (wh[2 * TILE :], wl[2 * TILE :])
    rr = lax.broadcasted_iota(jnp.int32, (TILE, TILE), 0)
    cc = lax.broadcasted_iota(jnp.int32, (TILE, TILE), 1)
    p0 = product(split(c0[0]), w00, mm_t)
    p0 = jnp.where((i_tile != 0) | (rr >= cc), p0, 0.0)
    panel[0, :, 0:TILE] = p0
    p0s = split(p0)
    ph[:, 0:TILE] = p0s[0]
    plo[:, 0:TILE] = p0s[1]
    rest = c1[0] - product(p0s, l10, mm_t)
    p1 = product(split(rest), w11, mm_t)
    p1 = jnp.where((i_tile > 1) | ((i_tile == 1) & (rr >= cc)), p1, 0.0)
    panel[0, :, TILE:] = p1
    p1s = split(p1)
    ph[:, TILE:] = p1s[0]
    plo[:, TILE:] = p1s[1]

    for n in range(4):
        t = n // 2
        j_tile = t * 16 + c
        alive = ((i_tile >= 2) & (j_tile >= 2)).astype(F32)
        mask = keep[i_tile, j_tile].astype(F32) * alive
        cols = slice(n * 256, (n + 1) * 256)
        acc = product((ph[...], plo[...]), (pth[:, cols], ptl[:, cols]), mm)
        for h in range(2):
            k = 2 * ((n % 2) * 2 + h) + t
            a = cov[0, :, k, :]
            schur[0, :, k, :] = a * mask - acc[:, h * 128 : (h + 1) * 128] * alive


def finish(keep, cov, cbuf, tbuf, w):
    return pl.pallas_call(
        finish_kernel,
        grid=(4,),
        out_shape=(
            jax.ShapeDtypeStruct((4, TILE, 8, 128), F32),
            jax.ShapeDtypeStruct((4, TILE, 2 * TILE), F32),
        ),
        in_specs=[
            pl.BlockSpec(memory_space=pltpu.SMEM),
            pl.BlockSpec((1, TILE, 8, 128), lambda q: (q, 0, 0, 0)),
            pl.BlockSpec((1, TILE, TILE), lambda q: (q, 0, 0)),
            pl.BlockSpec((1, TILE, TILE), lambda q: (q + 4, 0, 0)),
            pl.BlockSpec(memory_space=pltpu.VMEM),
            pl.BlockSpec(memory_space=pltpu.VMEM),
        ],
        out_specs=(
            pl.BlockSpec((1, TILE, 8, 128), lambda q: (q, 0, 0, 0)),
            pl.BlockSpec((1, TILE, 2 * TILE), lambda q: (q, 0, 0)),
        ),
        scratch_shapes=[
            pltpu.VMEM((3 * TILE, TILE), BF16),
            pltpu.VMEM((3 * TILE, TILE), BF16),
            pltpu.VMEM((2 * TILE, 2 * TILE), BF16),
            pltpu.VMEM((2 * TILE, 2 * TILE), BF16),
            pltpu.VMEM((TILE, 2 * TILE), BF16),
            pltpu.VMEM((TILE, 2 * TILE), BF16),
        ],
        compiler_params=pltpu.CompilerParams(vmem_limit_bytes=56 * 2**20),
        name="finish",
    )(keep, cov, cbuf, cbuf, tbuf, w)


def body(covariance, band_mask):
    x0 = covariance[:, :, 0, :]
    x1 = covariance[0, :, 1, :]
    cbuf, tbuf, w = exchange(x0, x1)
    cov = covariance.reshape(4, TILE, 2, 4, 128).transpose(0, 1, 3, 2, 4).reshape(4, TILE, 8, 128)
    schur, panels = finish(band_mask, cov, cbuf, tbuf, w)
    schur = schur.reshape(4, TILE, 4, 2, 128).transpose(0, 1, 3, 2, 4).reshape(4, TILE, 2, TILE)
    return (schur, panels)


def solution(mesh):
    return jax.shard_map(
        body,
        mesh=mesh,
        in_specs=(P(None, "row", None, "col"), P()),
        out_specs=(P(None, "row", None, "col"), P(None, "row", None)),
        check_vma=False,
    )
```

time: 892 us -> 531 us (0.60)
  Pallas kernels: 0 us -> 513 us
  waiting for transfers between devices: 431 us -> 0 us
  other arithmetic: 275 us -> 0 us
  matrix products: 74.4 us -> 0 us
  local copies, waits for them, and re-layouts: 82.3 us -> 17.3 us
  between operations: 20.1 us -> 0.66 us
    pallas_call x0 -> x2, Pallas kernels: none -> 513 us  [the longest x1 468 us: exchange(): pl.pallas_call(exchange_kernel, out_shape=(jax.ShapeDtypeStruct((12, TILE...]
    psum x6 -> x0, waiting for transfers between devices: 431 us -> none  [from_root(): return lax.psum(jnp.where(mine, value, jnp.zeros_like(value)), axis)]
    another operation x36 -> x0, other arithmetic: 243 us -> none  [the longest x29 158 us: make_panel(): factor = jnp.linalg.cholesky(diagonal)]
    another operation x26 -> x0, matrix products: 39.3 us -> none  [the longest x14 35.6 us: solve_below(): lax.linalg.triangular_solve(factor, rhs_block, left_side=True, lower=True)]
    dot_general x2 -> x0, matrix products: 35 us -> none  [outer_update(): jnp.einsum('mab,ncb->manc', row_part, col_part, precision=lax.Precision.H...]
    unnamed x14 -> x4, local copies, waits for them, and re-layouts: 34.5 us -> 6.37 us
    another operation x36 -> x0, local copies, waits for them, and re-layouts: 21.1 us -> none  [the longest x28 20.8 us: solve_below(): lax.linalg.triangular_solve(factor, rhs_block, left_side=True, lower=True)]
    transpose x4 -> x0, local copies, waits for them, and re-layouts: 20.3 us -> none  [solve_below(): rhs_block = jnp.transpose(column, (2, 0, 1)).reshape(TILE, count * TILE)]
  transfers between devices with their start and end apart: 6 -> 0, of which waited for: 6 -> 0; matrix products, arithmetic and copies ran while one was open for 3% -> 0% of each run, Pallas kernels for 0% -> 0%
where the time goes in v1:
time: 531 us
  Pallas kernels  513 us (97%)
  local copies, waits for them, and re-layouts  17.3 us (3%)
    pallas_call x1, Pallas kernels, exchange(): pl.pallas_call(exchange_kernel, out_shape=(jax.ShapeDtypeStruct((12, TILE...  468 us
    pallas_call x1, Pallas kernels, finish(): pl.pallas_call(finish_kernel, grid=(4,), out_shape=(jax.ShapeDtypeStruct(...  45.5 us

profile of v1, /device:TPU:45, one launch (start us, length us, event | category | flops | bytes accessed | tf_op | source)
XLA Modules:
  0.0 531.0 jit_solution(12480877661582579213)
XLA Ops:
  0.6 2.7 slice.7
  3.3 0.1 copy.13
  3.4 8.3 %slice.6 = f32[4,512,1,512]{3,2,1,0:T(1,128)} slice(f32[4,512,2,512]{3,2,1,0:T(2,128)} %param.2), slice={[0:4], [0:512], [0:1], [0:512]} | slice | bytes 8388608 | tf_op jit(solution)/shard_map/slice | solution.py:607
  11.7 4.7 copy.12
  16.3 467.6 %exchange.1 = (f32[12,512,512]{2,1,0:T(8,128)}, f32[2,2,512,512]{3,2,1,0:T(8,128)}, f32[1536,512]{1,0:T(8,128)S(1)}) custom-call(f32[4,512,512]{2,1,0:T(8,128)} %bitcast.18, f32[512,512]{1,0:T(8,128)S(1)} %bitcast.16), custom_call_target="tpu_custom_call" | custom-call | tf_op jit(solution)/shard_map/exchange/pallas_call | solution.py:470
  483.9 0.0 copy-start
  483.9 1.6 copy-done
  485.5 45.5 %finish.1 = (f32[4,512,8,128]{3,2,1,0:T(8,128)}, f32[4,512,1024]{2,1,0:T(8,128)}) custom-call(s32[32,32]{1,0:T(8,128)} %keep.1, f32[4,512,8,128]{3,2,1,0:T(8,128)} %bitcast.17, f32[12,512,512]{2,1,0:T(8,128)} %get-tuple-element.7.c0.c1, f32[12,512,512]{2,1,0:T(8,128)} %get-tuple-element.7.c0.c1, f32[2,2,512,512]{3,2,1,0:T(8,128)} %get-tuple-element.8.tb, ...), custom_call_target="tpu_custom_call" | custom-call | tf_op jit(solution)/shard_map/finish/pallas_call | solution.py:574
Async XLA Ops:
  483.9 1.7 copy-start

commit v2 on v1

--- a/solution.py
+++ b/solution.py
@@ -21,11 +21,13 @@
 }
 TREE_DEPTH = {0: 0, 4: 1, 7: 2, 8: 2, 5: 2, 11: 3, 6: 3, 1: 3, 3: 3, 9: 3, 12: 3, 10: 4, 2: 4, 13: 4, 15: 4, 14: 5}
 MAX_DEPTH = 5
-CHUNKS = 16
+CHUNKS = 8
 CROWS = TILE // CHUNKS
-TCHUNKS = 8
+TCHUNKS = 4
 TROWS = TILE // TCHUNKS
-WROWS = B // 4
+TRI = NB * (NB + 1) // 2
+FIRST = (0, TRI, TRI + NB * NB)
+PIECES = 2 * TRI + NB * NB
 
 
 def factor_block(rows):
@@ -76,7 +78,7 @@
     return lax.dot_general(a, b, (((1,), (1,)), ((), ())), precision=HIGH, preferred_element_type=F32)
 
 
-def factor_tile(m, w, base, publish):
+def factor_tile(m, w, first, send):
     rr = lax.broadcasted_iota(jnp.int32, (B, B), 0)
     cc = lax.broadcasted_iota(jnp.int32, (B, B), 1)
     cw = lax.broadcasted_iota(jnp.int32, (B, TILE), 1)
@@ -89,8 +91,14 @@
         row = dot_nn(inv, m[pl.ds(o, B), :])
         row = jnp.where(inside, jnp.concatenate([inv] * NB, axis=1), row)
         m[pl.ds(o, B), :] = row
-        w[pl.ds(pl.multiple_of(base + o, B), B), :] = jnp.where(cw < o + B, row, 0.0)
-        publish(k)
+
+        def publish(n, _):
+            piece = first + k * (k + 1) // 2 + n
+            w[piece] = m[pl.ds(o, B), pl.ds(pl.multiple_of(n * B, B), B)]
+            send(piece)
+            return 0
+
+        lax.fori_loop(0, k + 1, publish, 0)
 
         def update(i, _):
             oi = pl.multiple_of(i * B, B)
@@ -113,7 +121,7 @@
 
 
 def exchange_kernel(
-    x0, x1, cbuf, tbuf, wout, m, amat, w, csend, crecv, tsend, trecv, wsend, wrecv, asend, arecv, lsem
+    x0, x1, cbuf, tbuf, wout, m, amat, w, bounce, csend, crecv, tsend, trecv, wsend, wrecv, asend, arecv, lsem
 ):
     r = lax.axis_index("row")
     c = lax.axis_index("col")
@@ -270,7 +278,7 @@
 
         lax.fori_loop(0, TCHUNKS, go, 0)
         for t in range(2):
-            pltpu.make_async_copy(t_src[t], tbuf.at[core, t], lsem.at[1 + t]).start()
+            pltpu.make_async_copy(t_src[t], bounce.at[4 + t], lsem.at[1 + t]).start()
 
     for s in range(2):
 
@@ -278,46 +286,43 @@
         def _():
             send_all(s)
             for q in range(4):
-                pltpu.make_async_copy(x0.at[q], cbuf.at[4 * s + q], lsem.at[3 + q]).start()
-
-    w_on = []
-    for q in range(4):
-        _, _, flags = place[q]
-        on = [(flags[d] & (y == 0), around[(d + q) % 4]) if flags[d] is not None else None for d in range(4)]
-        if q % 2 == 0:
-            on.append((y < 3, y_next))
-        else:
-            on.append((y != 1, y_prev))
-        on.append((core == 0, sibling))
-        w_on.append(on)
-
-    def w_rows(block, q):
-        return pl.ds(pl.multiple_of(block * B + q * WROWS, WROWS), WROWS)
-
-    def w_forward(block, q):
-        for d, entry in enumerate(w_on[q]):
-            if entry is None:
-                continue
-            flag, dev = entry
+                pltpu.make_async_copy(x0.at[q], bounce.at[q], lsem.at[3 + q]).start()
+            for q in range(4):
+                pltpu.make_async_copy(x0.at[q], bounce.at[q], lsem.at[3 + q]).wait()
+                pltpu.make_async_copy(bounce.at[q], cbuf.at[4 * s + q], lsem.at[3 + q]).start()
+
+    @pl.when(t_source)
+    def _():
+        for t in range(2):
+            pltpu.make_async_copy(t_src[t], bounce.at[4 + t], lsem.at[1 + t]).wait()
+            pltpu.make_async_copy(bounce.at[4 + t], tbuf.at[core, t], lsem.at[1 + t]).start()
+
+    w_on = [
+        ((y == 0) & (z == 0) & (x < 2), around[0]),
+        ((y == 0) & (z == 0) & (x == 0), around[2]),
+        ((y == 0) & (z < 2), around[1]),
+        ((y == 0) & (z == 0), around[3]),
+        (y < 2, y_next),
+        (y == 0, y_prev),
+        (core == 0, sibling),
+    ]
+
+    def w_send(piece):
+        for d, (flag, dev) in enumerate(w_on):
 
             @pl.when(flag & (core == 0))
             def _():
                 pltpu.make_async_remote_copy(
-                    w.at[w_rows(block, q)], w.at[w_rows(block, q)], wsend.at[q, d], wrecv.at[block, q],
-                    device_id=dev, device_id_type=MESH,
+                    w.at[piece], w.at[piece], wsend.at[d], wrecv.at[piece], device_id=dev, device_id_type=MESH
                 ).start()
 
-    def w_wait(block, q):
-        pltpu.make_async_copy(w.at[w_rows(block, q)], w.at[w_rows(block, q)], wrecv.at[block, q]).wait()
-
-    def w_pass(mat):
-        def go(k, _):
-            for q in range(4):
-                w_wait(mat * NB + k, q)
-                w_forward(mat * NB + k, q)
-            return 0
-
-        lax.fori_loop(0, NB, go, 0)
+    def w_pass(begin, end):
+        def go(piece, _):
+            pltpu.make_async_copy(w.at[piece], w.at[piece], wrecv.at[piece]).wait()
+            w_send(piece)
+            return 0
+
+        lax.fori_loop(begin, end, go, 0)
 
     def c_wait(slot, chunk):
         pltpu.make_async_copy(cbuf.at[slot, crow(chunk)], cbuf.at[slot, crow(chunk)], crecv.at[slot, chunk]).wait()
@@ -329,22 +334,24 @@
     def _():
         first.wait()
 
-        def publish(base):
-            def go(k):
-                for q in range(4):
-                    w_forward(base + k, q)
-
-            return go
-
-        factor_tile(m, w, 0, publish(0))
+        factor_tile(m, w, FIRST[0], w_send)
+        big_r = lax.broadcasted_iota(jnp.int32, (TILE, TILE), 0)
+        big_c = lax.broadcasted_iota(jnp.int32, (TILE, TILE), 1)
+        inv00 = jnp.where(big_r // B >= big_c // B, m[...], 0.0)
         a10.wait_recv()
-        left = dot_nt(amat[0], w[0:TILE, :])
-        w[TILE : 2 * TILE, :] = left
-        for k in range(NB):
-            publish(NB)(k)
+        left = dot_nt(amat[0], inv00)
+        amat[0] = left
+
+        def publish(n, _):
+            rows, cols = (pl.ds(pl.multiple_of(v * B, B), B) for v in (n // NB, n % NB))
+            w[FIRST[1] + n] = amat[0, rows, cols]
+            w_send(FIRST[1] + n)
+            return 0
+
+        lax.fori_loop(0, NB * NB, publish, 0)
         a11.wait_recv()
         m[...] = amat[1] - dot_nt(left, left)
-        factor_tile(m, w, 2 * TILE, publish(2 * NB))
+        factor_tile(m, w, FIRST[2], w_send)
         for q in range(4):
 
             def drain(chunk, _):
@@ -382,18 +389,18 @@
                             csend_to(cbuf.at[8 + q], 8 + q, 4 + q, 4, (0, 0), chunk).start()
                             forward(cbuf.at[8 + q], s, q, 8 + q, 4 + q, 0, chunk, False)
 
-            @pl.when(k == CHUNKS - 1)
+            @pl.when(k == 5)
             def _():
-                w_pass(0)
-
-            @pl.when(k == CHUNKS + 1)
+                w_pass(FIRST[0], FIRST[1])
+
+            @pl.when(k == 7)
             def _():
-                w_pass(1)
+                w_pass(FIRST[1], FIRST[2])
 
             return 0
 
         lax.fori_loop(0, CHUNKS + MAX_DEPTH, go, 0)
-        w_pass(2)
+        w_pass(FIRST[2], PIECES)
 
     for t in range(2):
 
@@ -431,27 +438,23 @@
 
         pltpu.make_async_copy(tbuf.at[0, t], tbuf.at[0, t], tsend.at[t, 1]).wait()
 
-    for q in range(4):
-        for d, entry in enumerate(w_on[q]):
-            if entry is None:
-                continue
-
-            @pl.when(entry[0] & (core == 0))
-            def _():
-                rows = 3 * NB * WROWS
-                pltpu.make_async_copy(w.at[0:rows], w.at[0:rows], wsend.at[q, d]).wait()
+    for d, (flag, _) in enumerate(w_on):
+
+        @pl.when(flag & (core == 0))
+        def _():
+            pltpu.make_async_copy(w, w, wsend.at[d]).wait()
 
     @pl.when(t_source)
     def _():
         for t in range(2):
-            pltpu.make_async_copy(t_src[t], tbuf.at[core, t], lsem.at[1 + t]).wait()
+            pltpu.make_async_copy(bounce.at[4 + t], tbuf.at[core, t], lsem.at[1 + t]).wait()
 
     for s in range(2):
 
         @pl.when(source[s])
         def _():
             for q in range(4):
-                pltpu.make_async_copy(x0.at[q], cbuf.at[4 * s + q], lsem.at[3 + q]).wait()
+                pltpu.make_async_copy(bounce.at[q], cbuf.at[4 * s + q], lsem.at[3 + q]).wait()
 
     @pl.when(proxy)
     def _():
@@ -472,20 +475,21 @@
         out_shape=(
             jax.ShapeDtypeStruct((12, TILE, TILE), F32),
             jax.ShapeDtypeStruct((2, 2, TILE, TILE), F32),
-            jax.ShapeDtypeStruct((3 * TILE, TILE), F32),
+            jax.ShapeDtypeStruct((PIECES, B, B), F32),
         ),
         in_specs=[any_space, any_space],
         out_specs=(any_space, any_space, any_space),
         scratch_shapes=[
             pltpu.VMEM((TILE, TILE), F32),
             pltpu.VMEM((2, TILE, TILE), F32),
-            pltpu.VMEM((3 * TILE, TILE), F32),
+            pltpu.VMEM((PIECES, B, B), F32),
+            pltpu.VMEM((6, TILE, TILE), F32),
             dma((12, 5)),
             dma((12, CHUNKS)),
             dma((2, 2)),
             dma((2, 2, TCHUNKS)),
-            dma((4, 6)),
-            dma((3 * NB, 4)),
+            dma((7,)),
+            dma((PIECES,)),
             dma((2,)),
             dma((2,)),
             dma((8,)),
@@ -522,9 +526,16 @@
 
     @pl.when(q == 0)
     def _():
-        hi, lo = split(wo[...])
-        wh[...] = hi
-        wl[...] = lo
+        for mat in range(3):
+            for i in range(NB):
+                for j in range(NB):
+                    at = (slice(mat * TILE + i * B, mat * TILE + (i + 1) * B), slice(j * B, (j + 1) * B))
+                    if mat != 1 and j > i:
+                        wh[at] = jnp.zeros((B, B), BF16)
+                        wl[at] = jnp.zeros((B, B), BF16)
+                    else:
+                        piece = FIRST[mat] + (i * NB + j if mat == 1 else i * (i + 1) // 2 + j)
+                        wh[at], wl[at] = split(wo[piece])
         w00 = (wh[0:TILE], wl[0:TILE])
         l10 = (wh[TILE : 2 * TILE], wl[TILE : 2 * TILE])
         w11 = (wh[2 * TILE :], wl[2 * TILE :])

time: 531 us -> 212 us (0.40)
  the two profiles are of different devices: /device:TPU:45 before, /device:TPU:85 now
where the time goes in v2:
time: 212 us
  Pallas kernels  194 us (92%)
  local copies, waits for them, and re-layouts  17.1 us (8%)
    pallas_call x1, Pallas kernels, exchange(): pl.pallas_call(exchange_kernel, out_shape=(jax.ShapeDtypeStruct((12, TILE...  149 us
    pallas_call x1, Pallas kernels, finish(): pl.pallas_call(finish_kernel, grid=(4,), out_shape=(jax.ShapeDtypeStruct(...  45.3 us
    slice x1, local copies, waits for them, and re-layouts, body(): x0 = covariance[:, :, 0, :]  8.27 us
    unnamed x4, local copies, waits for them, and re-layouts  6.14 us

profile of v2, /device:TPU:85, one launch (start us, length us, event | category | flops | bytes accessed | tf_op | source)
XLA Modules:
  0.0 211.8 jit_solution(11402844973579125092)
XLA Ops:
  0.6 2.7 %slice.7 = f32[1,512,1,512]{3,2,1,0:T(1,128)S(1)} slice(f32[4,512,2,512]{3,2,1,0:T(2,128)} %param.2), slice={[0:1], [0:512], [1:2], [0:512]} | slice | bytes 2097152 | tf_op jit(solution)/shard_map/slice | solution.py:619
  3.3 0.1 copy.13
  3.4 8.3 %slice.6 = f32[4,512,1,512]{3,2,1,0:T(1,128)} slice(f32[4,512,2,512]{3,2,1,0:T(2,128)} %param.2), slice={[0:4], [0:512], [0:1], [0:512]} | slice | bytes 8388608 | tf_op jit(solution)/shard_map/slice | solution.py:618
  11.7 4.7 %copy.12 = f32[4,512,1,512]{3,1,0,2:T(8,128)} copy(f32[4,512,1,512]{3,2,1,0:T(1,128)} %slice.6) | data formatting | bytes 8388608
  16.3 148.7 %exchange.1 = (f32[12,512,512]{2,1,0:T(8,128)}, f32[2,2,512,512]{3,2,1,0:T(8,128)}, f32[36,128,128]{2,1,0:T(8,128)S(1)}) custom-call(f32[4,512,512]{2,1,0:T(8,128)} %bitcast.18, f32[512,512]{1,0:T(8,128)S(1)} %bitcast.16), custom_call_target="tpu_custom_call" | custom-call | tf_op jit(solution)/shard_map/exchange/pallas_call | solution.py:473
  165.0 0.0 copy-start
  165.0 1.4 copy-done
  166.4 45.3 %finish.1 = (f32[4,512,8,128]{3,2,1,0:T(8,128)}, f32[4,512,1024]{2,1,0:T(8,128)}) custom-call(s32[32,32]{1,0:T(8,128)} %keep.1, f32[4,512,8,128]{3,2,1,0:T(8,128)} %bitcast.17, f32[12,512,512]{2,1,0:T(8,128)} %get-tuple-element.7.c0.c1, f32[12,512,512]{2,1,0:T(8,128)} %get-tuple-element.7.c0.c1, f32[2,2,512,512]{3,2,1,0:T(8,128)} %get-tuple-element.8.tb, ...), custom_call_target="tpu_custom_call" | custom-call | tf_op jit(solution)/shard_map/finish/pallas_call | solution.py:585
Async XLA Ops:
  165.0 1.4 copy-start

commit v3 on v2

--- a/solution.py
+++ b/solution.py
@@ -271,12 +271,15 @@
 
     @pl.when(t_source)
     def _():
-        def go(chunk, _):
-            for t in range(2):
-                t_forward(t_src[t], t, chunk)
-            return 0
-
-        lax.fori_loop(0, TCHUNKS, go, 0)
+        @pl.when(root)
+        def _():
+            def go(chunk, _):
+                for t in range(2):
+                    t_forward(t_src[t], t, chunk)
+                return 0
+
+            lax.fori_loop(0, TCHUNKS, go, 0)
+
         for t in range(2):
             pltpu.make_async_copy(t_src[t], bounce.at[4 + t], lsem.at[1 + t]).start()
 
@@ -284,7 +287,12 @@
 
         @pl.when(source[s])
         def _():
-            send_all(s)
+            if s == 0:
+
+                @pl.when(root)
+                def _():
+                    send_all(s)
+
             for q in range(4):
                 pltpu.make_async_copy(x0.at[q], bounce.at[q], lsem.at[3 + q]).start()
             for q in range(4):
@@ -297,32 +305,62 @@
             pltpu.make_async_copy(t_src[t], bounce.at[4 + t], lsem.at[1 + t]).wait()
             pltpu.make_async_copy(bounce.at[4 + t], tbuf.at[core, t], lsem.at[1 + t]).start()
 
-    w_on = [
-        ((y == 0) & (z == 0) & (x < 2), around[0]),
-        ((y == 0) & (z == 0) & (x == 0), around[2]),
-        ((y == 0) & (z < 2), around[1]),
-        ((y == 0) & (z == 0), around[3]),
-        (y < 2, y_next),
-        (y == 0, y_prev),
-        (core == 0, sibling),
-    ]
-
-    def w_send(piece):
-        for d, (flag, dev) in enumerate(w_on):
+    w_on, w_depth = [], []
+    for q in range(4):
+        _, depth, flags = place[q]
+        on = [(flags[d] & (y == 0), around[(d + q) % 4]) if flags[d] is not None else None for d in range(4)]
+        on.append((y < 3, y_next) if q % 2 == 0 else (y != 1, y_prev))
+        on.append((core == 0, sibling))
+        w_on.append(on)
+        w_depth.append(depth + t_depth[q % 2])
+
+    def w_send(n, q):
+        for d, entry in enumerate(w_on[q]):
+            if entry is None:
+                continue
+            flag, dev = entry
 
             @pl.when(flag & (core == 0))
             def _():
                 pltpu.make_async_remote_copy(
-                    w.at[piece], w.at[piece], wsend.at[d], wrecv.at[piece], device_id=dev, device_id_type=MESH
+                    w.at[4 * n + q], w.at[4 * n + q], wsend.at[q, d], wrecv.at[4 * n + q],
+                    device_id=dev, device_id_type=MESH,
                 ).start()
 
+    def w_send_piece(piece):
+        for q in range(4):
+
+            @pl.when(piece % 4 == q)
+            def _():
+                w_send(piece // 4, q)
+
+    def w_wait(piece):
+        pltpu.make_async_copy(w.at[piece], w.at[piece], wrecv.at[piece]).wait()
+
+    w_steps = PIECES // 4 + MAX_DEPTH + 3
+
     def w_pass(begin, end):
-        def go(piece, _):
-            pltpu.make_async_copy(w.at[piece], w.at[piece], wrecv.at[piece]).wait()
-            w_send(piece)
+        def go(k, _):
+            for q in range(4):
+                n = k - w_depth[q]
+
+                @pl.when((n >= 0) & (n < PIECES // 4) & (core == 0))
+                def _():
+                    w_wait(4 * n + q)
+                    w_send(n, q)
+
             return 0
 
         lax.fori_loop(begin, end, go, 0)
+
+    def w_rest():
+        @pl.when(core == 1)
+        def _():
+            def go(piece, _):
+                w_wait(piece)
+                return 0
+
+            lax.fori_loop(0, PIECES, go, 0)
 
     def c_wait(slot, chunk):
         pltpu.make_async_copy(cbuf.at[slot, crow(chunk)], cbuf.at[slot, crow(chunk)], crecv.at[slot, chunk]).wait()
@@ -334,7 +372,7 @@
     def _():
         first.wait()
 
-        factor_tile(m, w, FIRST[0], w_send)
+        factor_tile(m, w, FIRST[0], w_send_piece)
         big_r = lax.broadcasted_iota(jnp.int32, (TILE, TILE), 0)
         big_c = lax.broadcasted_iota(jnp.int32, (TILE, TILE), 1)
         inv00 = jnp.where(big_r // B >= big_c // B, m[...], 0.0)
@@ -345,13 +383,13 @@
         def publish(n, _):
             rows, cols = (pl.ds(pl.multiple_of(v * B, B), B) for v in (n // NB, n % NB))
             w[FIRST[1] + n] = amat[0, rows, cols]
-            w_send(FIRST[1] + n)
+            w_send_piece(FIRST[1] + n)
             return 0
 
         lax.fori_loop(0, NB * NB, publish, 0)
         a11.wait_recv()
         m[...] = amat[1] - dot_nt(left, left)
-        factor_tile(m, w, FIRST[2], w_send)
+        factor_tile(m, w, FIRST[2], w_send_piece)
         for q in range(4):
 
             def drain(chunk, _):
@@ -371,6 +409,10 @@
                     t_wait(core, t, chunk)
                     t_forward(tbuf.at[core, t], t, chunk)
 
+                @pl.when((chunk < TCHUNKS) & (y == 0))
+                def _():
+                    t_forward(t_src[t], t, chunk)
+
             for s in range(2):
                 for q in range(4):
                     _, depth, _ = place[4 * s + q]
@@ -380,6 +422,15 @@
                     def _():
                         c_wait(4 * s + q, chunk)
                         forward(cbuf.at[4 * s + q], s, q, 4 * s + q, 4 * s + q, r, chunk, s == 1)
+
+                    @pl.when((chunk < CHUNKS) & source[s])
+                    def _():
+                        d = 0
+                        col = around[q][1]
+                        away = (s == 1) & (col == 0) & (r == 0)
+                        csend_to(
+                            x0.at[q], 4 * s + q, jnp.where(away, 8 + q, 4 * s + q), d, (jnp.where(away, 1, r), col), chunk
+                        ).start()
 
                     if s == 1:
 
@@ -389,18 +440,15 @@
                             csend_to(cbuf.at[8 + q], 8 + q, 4 + q, 4, (0, 0), chunk).start()
                             forward(cbuf.at[8 + q], s, q, 8 + q, 4 + q, 0, chunk, False)
 
-            @pl.when(k == 5)
+            @pl.when(k >= 6)
             def _():
-                w_pass(FIRST[0], FIRST[1])
-
-            @pl.when(k == 7)
-            def _():
-                w_pass(FIRST[1], FIRST[2])
+                w_pass(2 * (k - 6), 2 * (k - 6) + 2)
 
             return 0
 
         lax.fori_loop(0, CHUNKS + MAX_DEPTH, go, 0)
-        w_pass(FIRST[2], PIECES)
+        w_pass(2 * (CHUNKS + MAX_DEPTH - 6), w_steps)
+        w_rest()
 
     for t in range(2):
 
@@ -438,11 +486,14 @@
 
         pltpu.make_async_copy(tbuf.at[0, t], tbuf.at[0, t], tsend.at[t, 1]).wait()
 
-    for d, (flag, _) in enumerate(w_on):
-
-        @pl.when(flag & (core == 0))
-        def _():
-            pltpu.make_async_copy(w, w, wsend.at[d]).wait()
+    for q in range(4):
+        for d, entry in enumerate(w_on[q]):
+            if entry is None:
+                continue
+
+            @pl.when(entry[0] & (core == 0))
+            def _():
+                pltpu.make_async_copy(w.at[0 : PIECES // 4], w.at[0 : PIECES // 4], wsend.at[q, d]).wait()
 
     @pl.when(t_source)
     def _():
@@ -488,19 +539,44 @@
             dma((12, CHUNKS)),
             dma((2, 2)),
             dma((2, 2, TCHUNKS)),
-            dma((7,)),
+            dma((4, 6)),
             dma((PIECES,)),
             dma((2,)),
             dma((2,)),
             dma((8,)),
         ],
         compiler_params=pltpu.CompilerParams(
-            collective_id=0, has_side_effects=True, vmem_limit_bytes=48 * 2**20
+            collective_id=0, has_side_effects=True, vmem_limit_bytes=60 * 2**20
         ),
         name="exchange",
     )(x0, x1)
 
 
+def pick_kernel(cov, x0, x1):
+    for k in range(NB):
+        x0[0, :, k * B : (k + 1) * B] = cov[0, :, 2 * k, :]
+
+    @pl.when(pl.program_id(0) == 0)
+    def _():
+        for k in range(NB):
+            x1[:, k * B : (k + 1) * B] = cov[0, :, 2 * k + 1, :]
+
+
+def pick(cov):
+    return pl.pallas_call(
+        pick_kernel,
+        grid=(4,),
+        out_shape=(jax.ShapeDtypeStruct((4, TILE, TILE), F32), jax.ShapeDtypeStruct((TILE, TILE), F32)),
+        in_specs=[pl.BlockSpec((1, TILE, 8, 128), lambda q: (q, 0, 0, 0))],
+        out_specs=(
+            pl.BlockSpec((1, TILE, TILE), lambda q: (q, 0, 0)),
+            pl.BlockSpec((TILE, TILE), lambda q: (0, 0)),
+        ),
+        compiler_params=pltpu.CompilerParams(vmem_limit_bytes=60 * 2**20),
+        name="pick",
+    )(cov)
+
+
 def split(a):
     hi = a.astype(BF16)
     return hi, (a - hi.astype(F32)).astype(BF16)
@@ -516,6 +592,18 @@
 
 def product(a, b, dot):
     return dot(a[0], b[0]) + (dot(a[0], b[1]) + dot(a[1], b[0]))
+
+
+def lower_product(w, b):
+    half = TILE // 2
+    top = product([v[:half, :half] for v in w], [v[:half] for v in b], mm)
+    return jnp.concatenate([top, product([v[half:] for v in w], b, mm)], axis=0)
+
+
+def product_lower(a, w):
+    half = TILE // 2
+    left = product([v[:, :half] for v in a], [v[:half, :half] for v in w], mm_t)
+    return jnp.concatenate([left, product(a, [v[half:] for v in w], mm_t)], axis=1)
 
 
 def finish_kernel(keep, cov, c0, c1, tb, wo, schur, panel, wh, wl, pth, ptl, ph, plo):
@@ -541,11 +629,11 @@
         w11 = (wh[2 * TILE :], wl[2 * TILE :])
         for t in range(2):
             cols = slice(t * TILE, (t + 1) * TILE)
-            p0 = split(product(w00, split(tb[0, t]), mm))
+            p0 = split(lower_product(w00, split(tb[0, t])))
             pth[0:TILE, cols] = p0[0]
             ptl[0:TILE, cols] = p0[1]
             rest = tb[1, t] - product(l10, p0, mm)
-            p1 = split(product(w11, split(rest), mm))
+            p1 = split(lower_product(w11, split(rest)))
             pth[TILE:, cols] = p1[0]
             ptl[TILE:, cols] = p1[1]
 
@@ -554,14 +642,14 @@
     w11 = (wh[2 * TILE :], wl[2 * TILE :])
     rr = lax.broadcasted_iota(jnp.int32, (TILE, TILE), 0)
     cc = lax.broadcasted_iota(jnp.int32, (TILE, TILE), 1)
-    p0 = product(split(c0[0]), w00, mm_t)
+    p0 = product_lower(split(c0[0]), w00)
     p0 = jnp.where((i_tile != 0) | (rr >= cc), p0, 0.0)
     panel[0, :, 0:TILE] = p0
     p0s = split(p0)
     ph[:, 0:TILE] = p0s[0]
     plo[:, 0:TILE] = p0s[1]
     rest = c1[0] - product(p0s, l10, mm_t)
-    p1 = product(split(rest), w11, mm_t)
+    p1 = product_lower(split(rest), w11)
     p1 = jnp.where((i_tile > 1) | ((i_tile == 1) & (rr >= cc)), p1, 0.0)
     panel[0, :, TILE:] = p1
     p1s = split(p1)
@@ -615,10 +703,9 @@
 
 
 def body(covariance, band_mask):
-    x0 = covariance[:, :, 0, :]
-    x1 = covariance[0, :, 1, :]
+    cov = covariance.reshape(4, TILE, 2, 4, 128).transpose(0, 1, 3, 2, 4).reshape(4, TILE, 8, 128)
+    x0, x1 = pick(cov)
     cbuf, tbuf, w = exchange(x0, x1)
-    cov = covariance.reshape(4, TILE, 2, 4, 128).transpose(0, 1, 3, 2, 4).reshape(4, TILE, 8, 128)
     schur, panels = finish(band_mask, cov, cbuf, tbuf, w)
     schur = schur.reshape(4, TILE, 4, 2, 128).transpose(0, 1, 3, 2, 4).reshape(4, TILE, 2, TILE)
     return (schur, panels)

time: 212 us -> 170 us (0.80)
  the two profiles are of different devices: /device:TPU:85 before, /device:TPU:45 now
where the time goes in v3:
time: 170 us; the launch traced here: 169 us
  Pallas kernels  169 us (99%)
    pallas_call x1, Pallas kernels, exchange(): pl.pallas_call(exchange_kernel, out_shape=(jax.ShapeDtypeStruct((12, TILE...  116 us
    pallas_call x1, Pallas kernels, finish(): pl.pallas_call(finish_kernel, grid=(4,), out_shape=(jax.ShapeDtypeStruct(...  45.1 us
    pallas_call x1, Pallas kernels, pick(): pl.pallas_call(pick_kernel, grid=(4,), out_shape=(jax.ShapeDtypeStruct((4...  7.59 us

profile of v3, /device:TPU:45, one launch (start us, length us, event | category | flops | bytes accessed | tf_op | source)
XLA Modules:
  0.0 169.4 jit_solution(7117055858634593159)
XLA Ops:
  0.6 7.6 %pick.1 = (f32[4,512,512]{2,1,0:T(8,128)}, f32[512,512]{1,0:T(8,128)}) custom-call(f32[4,512,8,128]{3,2,1,0:T(8,128)} %bitcast.10), custom_call_target="tpu_custom_call" | custom-call | tf_op jit(solution)/shard_map/pick/pallas_call | solution.py:566
  8.2 116.1 %exchange.1 = (f32[12,512,512]{2,1,0:T(8,128)}, f32[2,2,512,512]{3,2,1,0:T(8,128)}, f32[36,128,128]{2,1,0:T(8,128)}) custom-call(f32[4,512,512]{2,1,0:T(8,128)} %get-tuple-element.9.x0, f32[512,512]{1,0:T(8,128)} %get-tuple-element.10.x1), custom_call_target="tpu_custom_call" | custom-call | tf_op jit(solution)/shard_map/exchange/pallas_call | solution.py:524
  124.3 45.1 %finish.1 = (f32[4,512,8,128]{3,2,1,0:T(8,128)}, f32[4,512,1024]{2,1,0:T(8,128)}) custom-call(s32[32,32]{1,0:T(8,128)} %keep.1, f32[4,512,8,128]{3,2,1,0:T(8,128)} %bitcast.11, f32[12,512,512]{2,1,0:T(8,128)} %get-tuple-element.11.c0.c1, f32[12,512,512]{2,1,0:T(8,128)} %get-tuple-element.11.c0.c1, f32[2,2,512,512]{3,2,1,0:T(8,128)} %get-tuple-element.12.tb, ...), custom_call_target="tpu_custom_call" | custom-call | tf_op jit(solution)/shard_map/finish/pallas_call | solution.py:673

commit v4 on v3

--- a/solution.py
+++ b/solution.py
@@ -440,14 +440,14 @@
                             csend_to(cbuf.at[8 + q], 8 + q, 4 + q, 4, (0, 0), chunk).start()
                             forward(cbuf.at[8 + q], s, q, 8 + q, 4 + q, 0, chunk, False)
 
-            @pl.when(k >= 6)
+            @pl.when(k >= 5)
             def _():
-                w_pass(2 * (k - 6), 2 * (k - 6) + 2)
+                w_pass(2 * (k - 5), 2 * (k - 5) + 2)
 
             return 0
 
         lax.fori_loop(0, CHUNKS + MAX_DEPTH, go, 0)
-        w_pass(2 * (CHUNKS + MAX_DEPTH - 6), w_steps)
+        w_pass(2 * (CHUNKS + MAX_DEPTH - 5), w_steps)
         w_rest()
 
     for t in range(2):

time: 170 us -> 168 us (0.988)
  Pallas kernels: 169 us -> 167 us
    pallas_call x1, Pallas kernels: 116 us -> 114 us  [exchange(): pl.pallas_call(exchange_kernel, out_shape=(jax.ShapeDtypeStruct((12, TILE...]
where the time goes in v4:
time: 168 us; the launch traced here: 167 us
  Pallas kernels  167 us (99%)
    pallas_call x1, Pallas kernels, exchange(): pl.pallas_call(exchange_kernel, out_shape=(jax.ShapeDtypeStruct((12, TILE...  114 us
    pallas_call x1, Pallas kernels, finish(): pl.pallas_call(finish_kernel, grid=(4,), out_shape=(jax.ShapeDtypeStruct(...  45.1 us
    pallas_call x1, Pallas kernels, pick(): pl.pallas_call(pick_kernel, grid=(4,), out_shape=(jax.ShapeDtypeStruct((4...  7.59 us

profile of v4, /device:TPU:45, one launch (start us, length us, event | category | flops | bytes accessed | tf_op | source)
XLA Modules:
  0.0 167.4 jit_solution(15896415408066341622)
XLA Ops:
  0.6 7.6 %pick.1 = (f32[4,512,512]{2,1,0:T(8,128)}, f32[512,512]{1,0:T(8,128)}) custom-call(f32[4,512,8,128]{3,2,1,0:T(8,128)} %bitcast.10), custom_call_target="tpu_custom_call" | custom-call | tf_op jit(solution)/shard_map/pick/pallas_call | solution.py:566
  8.2 114.1 %exchange.1 = (f32[12,512,512]{2,1,0:T(8,128)}, f32[2,2,512,512]{3,2,1,0:T(8,128)}, f32[36,128,128]{2,1,0:T(8,128)}) custom-call(f32[4,512,512]{2,1,0:T(8,128)} %get-tuple-element.9.x0, f32[512,512]{1,0:T(8,128)} %get-tuple-element.10.x1), custom_call_target="tpu_custom_call" | custom-call | tf_op jit(solution)/shard_map/exchange/pallas_call | solution.py:524
  122.4 45.1 %finish.1 = (f32[4,512,8,128]{3,2,1,0:T(8,128)}, f32[4,512,1024]{2,1,0:T(8,128)}) custom-call(s32[32,32]{1,0:T(8,128)} %keep.1, f32[4,512,8,128]{3,2,1,0:T(8,128)} %bitcast.11, f32[12,512,512]{2,1,0:T(8,128)} %get-tuple-element.11.c0.c1, f32[12,512,512]{2,1,0:T(8,128)} %get-tuple-element.11.c0.c1, f32[2,2,512,512]{3,2,1,0:T(8,128)} %get-tuple-element.12.tb, ...), custom_call_target="tpu_custom_call" | custom-call | tf_op jit(solution)/shard_map/finish/pallas_call | solution.py:673
